TPU v7x, 32 devices: a whole 2x2x4 slice. The times are simulated.
32 devices in a mesh: dp: 8 (over z, x), mp: 4 (over y, core).
Axes of the slice: x: 2, y: 2, z: 4, core: 2. Of those that a mesh axis runs over, the one named last changes fastest.
Arguments:
- partials: bfloat16 [8, 8, 640, 1024], P('dp', None, None, 'mp'), may hold values from -6 to 6
- owner: int32 [8], replicated, may hold values from 0 to 7, as said below
- rowblock: int32 [8, 8], replicated, may hold values from 0 to 7, each once within a row
- factor: float32 [8, 640, 2, 640], P('dp', 'mp'), as said below
- basis: float32 [8, 640, 2, 640], P('dp', 'mp'), may hold values from -0.25 to 0.25
- moment1: float32 [8, 2, 640, 1024], P('dp', None, None, 'mp'), may hold values from -1.5 to 1.5
- moment2: float32 [8, 2, 640, 1024], P('dp', None, None, 'mp'), may hold values from 0.001 to 0.02
- master: float32 [8, 2, 640, 1024], P('dp', None, None, 'mp'), may hold values from -6 to 6
Outputs:
- train_weights: float32 [8, 8, 80, 1024], P(None, 'dp', None, 'mp')
- new_basis: float32 [8, 640, 2, 640], P('dp', 'mp')
Inputs may be any that keep to these rules, and one draw needn't show every extreme that they name: `owner`: each data group owns at most 2 matrices and one owns exactly 2; the first and the last data group each own a matrix. `rowblock`: each row is a permutation of the data groups' row blocks. `factor`: symmetric in its two 640 dimensions.
All inputs are finite; a program needn't handle non-finite values.
Results may differ from a plain program's by a relative error of at most 0.0003.
Values sent between devices are 32-bit elements; how exact they have to be, the bound alone decides.
A program may use at most 128 MiB of HBM per device.

v0:
```python
import jax
import jax.numpy as jnp
from jax import lax
from jax.sharding import PartitionSpec as P

NS_ITERS = 4


def body(partials, owner, rowblock, factor, basis, moment1, moment2, master):
    top_precision = lax.Precision.HIGHEST
    groups = lax.axis_size("dp")
    my_index = lax.axis_index("dp")
    count = owner.shape[0]
    slots = factor.shape[2]
    order = jnp.arange(count)
    same = owner[:, None] == owner[None, :]
    slot = jnp.sum((same & (order[None, :] < order[:, None])).astype(jnp.int32), axis=1)
    hits = (owner[None, None, :] == jnp.arange(groups)[:, None, None]) & (
        slot[None, None, :] == jnp.arange(slots)[None, :, None]
    )
    hit_float = hits.astype(jnp.float32)
    my_hits = lax.dynamic_index_in_dim(hit_float, my_index, 0, keepdims=False)
    valid = jnp.sum(my_hits, axis=1)
    my_matrix = jnp.sum(my_hits.astype(jnp.int32) * order[None, :], axis=1)
    local = partials[0].astype(jnp.float32)
    summed = lax.psum(local, "dp")
    query_gradient = jnp.einsum("sm,mdc->sdc", my_hits, summed, precision=top_precision) / groups
    complete_eigvectors = lax.all_gather(basis[0], "mp", axis=0, tiled=True)
    turned_gradient = jnp.einsum(
        "tnu,ntg->nug", complete_eigvectors, query_gradient, precision=top_precision
    )
    leading_moment = 0.9 * moment1[0] + 0.1 * turned_gradient
    trailing_moment = 0.95 * moment2[0] + 0.05 * turned_gradient * turned_gradient
    direction = jnp.einsum(
        "uoh,ohz->ouz",
        complete_eigvectors,
        leading_moment / (jnp.sqrt(trailing_moment) + 1e-08),
        precision=top_precision,
    )
    held = master[0]
    weights = held - 0.1 * (direction + 0.1 * held)
    outer = lax.psum_scatter(
        jnp.einsum("src,sec->rse", query_gradient, query_gradient, precision=top_precision),
        "mp",
        scatter_dimension=0,
        tiled=True,
    )
    statistic = 0.95 * factor[0] + 0.05 * outer
    power = jnp.einsum("rse,esf->rsf", statistic, complete_eigvectors, precision=top_precision)
    total = lax.psum(jnp.sum(power * power, axis=(0, 2)), "mp")
    iterate = power / jnp.sqrt(total + 1e-06)[None, :, None]
    for step in range(NS_ITERS):
        gathered = lax.all_gather(iterate, "mp", axis=0, tiled=True)
        inner = jnp.einsum("rsf,esf->rse", iterate, gathered, precision=top_precision)
        inner_whole = lax.all_gather(inner, "mp", axis=0, tiled=True)
        squared = jnp.einsum("rse,esg->rsg", inner, inner_whole, precision=top_precision)
        merged_update = -4.775 * inner + 2.0315 * squared
        iterate = 3.4445 * iterate + jnp.einsum(
            "rse,esf->rsf", merged_update, gathered, precision=top_precision
        )
    new_basis = (iterate * valid[None, :, None])[None]
    block_rows = weights.shape[1] // groups
    columns = weights.shape[2]
    shaped = weights.reshape(slots, groups, block_rows, columns)
    chosen = jnp.take(rowblock, my_matrix, axis=0)
    sending = jnp.take_along_axis(shaped, chosen[:, :, None, None], axis=1)
    received = lax.all_to_all(sending, "dp", split_axis=1, concat_axis=0, tiled=True)
    train_weights = jnp.take(received, owner * slots + slot, axis=0)
    return (train_weights, new_basis)


def solution(mesh):
    placed = (
        P("dp", None, None, "mp"),
        P(),
        P(),
        P("dp", "mp", None, None),
        P("dp", "mp", None, None),
        P("dp", None, None, "mp"),
        P("dp", None, None, "mp"),
        P("dp", None, None, "mp"),
    )
    return jax.shard_map(
        body,
        mesh=mesh,
        in_specs=placed,
        out_specs=(P(None, "dp", None, "mp"), P("dp", "mp", None, None)),
        check_vma=False,
    )
```

profile of v0, /device:TPU:1, one launch (start us, length us, event | category | flops | bytes accessed | tf_op | source)
XLA Modules:
  0.0 667.5 jit_solution(10541484444429350578)
XLA Ops:
  7.2 5.6 bitcast_convert_fusion
  12.9 0.6 copy-done.17
  13.7 185.4 %all-reduce.4.cloned.1.call-done = f32[8,640,256]{2,0,1:T(8,128)} async-done(((f32[8,640,256]{2,0,1:T(8,128)}), f32[8,640,256]{2,0,1:T(8,128)}) %all-reduce.4.cloned.1.call-update) | async-done | bytes 5242896 | tf_op jit(solution)/shard_map/psum | solution.py:26
  199.1 5.0 fusion.55
  204.1 1.1 copy-done.10
  205.1 3.5 convolution_bitcast_fusion
  208.7 6.5 copy.55
  215.3 1.1 copy-done.15
  216.4 0.9 copy.50
  217.6 0.6 dynamic-slice
  218.9 66.0 %all-reduce.6.cloned.1.call-done = f32[640,2,640]{2,1,0:T(2,128)} async-done(((f32[640,2,640]{2,1,0:T(2,128)}), f32[640,2,640]{2,1,0:T(2,128)}) %all-reduce.6.cloned.1.call-update) | async-done | bytes 3276816
  284.9 2.0 fusion.44
  286.9 30.1 %all-gather.27.cloned.1.call-done = f32[1,640,2,640]{3,1,2,0:T(8,128)} async-done(((f32[1,160,2,640]{3,1,2,0:T(8,128)}), f32[1,640,2,640]{3,1,2,0:T(8,128)}) %all-gather.27.cloned.1.call-update) | async-done | bytes 3276816 | tf_op jit(solution)/shard_map/all_gather | solution.py:28
  317.0 4.7 multiply_reduce_fusion
  321.7 5.3 psum.15
  326.9 1.0 divide_bitcast_fusion
  328.0 31.1 %all-gather.11.cloned.1.call-done = f32[640,2,640]{2,0,1:T(8,128)} async-done(((f32[160,2,640]{2,0,1:T(8,128)}), f32[640,2,640]{2,0,1:T(8,128)}) %all-gather.11.cloned.1.call-update) | async-done | bytes 3276816 | tf_op jit(solution)/shard_map/all_gather | solution.py:53
  359.1 6.5 convolution_bitcast_fusion.8
  366.1 29.0 %all-gather.13.cloned.1.call-done = f32[640,2,640]{2,0,1:T(8,128)} async-done(((f32[160,2,640]{2,0,1:T(8,128)}), f32[640,2,640]{2,0,1:T(8,128)}) %all-gather.13.cloned.1.call-update) | async-done | bytes 3276816 | tf_op jit(solution)/shard_map/all_gather | solution.py:55
  395.1 5.3 fusion.43
  400.4 3.7 fusion.41
  404.2 29.4 %all-gather.15.cloned.1.call-done = f32[640,2,640]{2,0,1:T(8,128)} async-done(((f32[160,2,640]{2,0,1:T(8,128)}), f32[640,2,640]{2,0,1:T(8,128)}) %all-gather.15.cloned.1.call-update) | async-done | bytes 3276816 | tf_op jit(solution)/shard_map/all_gather | solution.py:53
  433.6 6.5 convolution_bitcast_fusion.6
  440.4 29.2 %all-gather.17.cloned.1.call-done = f32[640,2,640]{2,0,1:T(8,128)} async-done(((f32[160,2,640]{2,0,1:T(8,128)}), f32[640,2,640]{2,0,1:T(8,128)}) %all-gather.17.cloned.1.call-update) | async-done | bytes 3276816 | tf_op jit(solution)/shard_map/all_gather | solution.py:55
  469.6 5.3 fusion.40
  474.9 3.7 fusion.38
  478.7 29.4 %all-gather.19.cloned.1.call-done = f32[640,2,640]{2,0,1:T(8,128)} async-done(((f32[160,2,640]{2,0,1:T(8,128)}), f32[640,2,640]{2,0,1:T(8,128)}) %all-gather.19.cloned.1.call-update) | async-done | bytes 3276816 | tf_op jit(solution)/shard_map/all_gather | solution.py:53
  508.1 6.5 convolution_bitcast_fusion.4
  514.7 29.4 %all-gather.21.cloned.1.call-done = f32[640,2,640]{2,0,1:T(8,128)} async-done(((f32[160,2,640]{2,0,1:T(8,128)}), f32[640,2,640]{2,0,1:T(8,128)}) %all-gather.21.cloned.1.call-update) | async-done | bytes 3276816 | tf_op jit(solution)/shard_map/all_gather | solution.py:55
  544.1 5.3 fusion.37
  549.4 3.7 fusion.35
  553.4 29.2 %all-gather.23.cloned.1.call-done = f32[640,2,640]{2,0,1:T(8,128)} async-done(((f32[160,2,640]{2,0,1:T(8,128)}), f32[640,2,640]{2,0,1:T(8,128)}) %all-gather.23.cloned.1.call-update) | async-done | bytes 3276816 | tf_op jit(solution)/shard_map/all_gather | solution.py:53
  582.5 6.5 convolution_bitcast_fusion.2
  590.0 1.5 copy.46
  591.5 2.9 copy.47
  594.4 2.9 copy.52
  597.5 5.7 fusion.6
  603.3 6.1 fusion.18
  609.3 1.7 copy.53
  611.0 0.6 gather_fusion.2
  611.7 1.2 copy_select_fusion
  612.9 5.4 all-to-all-start
  618.5 30.8 %all-to-all-done = f32[2,8,80,256]{3,2,0,1:T(8,128)S(1)} async-done(((f32[2,8,80,256]{3,2,0,1:T(8,128)}), f32[2,8,80,256]{3,2,0,1:T(8,128)S(1)}, u32[]{:S(2)}, u32[]{:S(2)}) %all-to-all-start) | async-done | bytes 1310752 | tf_op jit(solution)/shard_map/all_to_all | solution.py:67
  649.3 0.6 gather_fusion.1
  649.9 0.9 fusion.46
  650.8 5.3 fusion.34
  656.2 2.9 fusion.32
  659.1 1.5 copy.58
  (75 shorter events, 3.1 us)
Async XLA Ops:
  7.2 582.1 %copy-start = (s32[8,8]{1,0:T(8,128)S(1)}, s32[8,8]{1,0:T(8,128)}, u32[]{:S(2)}) copy-start(s32[8,8]{1,0:T(8,128)} %param.10) | copy-start | bytes 772
  7.2 191.9 %all-reduce.4.cloned.1.call-start = ((), (), s32[]{:S(2)}) async-start(), calls=%async_computation.1 | async-start | bytes 10485760 | tf_op jit(solution)/shard_map/psum | solution.py:26
  12.9 0.7 copy-start.17
  12.9 272.0 %all-reduce.6.cloned.1.call-start = ((), (), s32[]{:S(2)}) async-start(), calls=%async_computation.11 | async-start | bytes 6553600
  204.1 1.1 copy-start.10
  215.2 1.1 copy-start.15
  215.2 2.4 copy-start.18
  215.2 69.7 %copy-start.16 = (f32[1,160,2,640]{3,2,1,0:T(2,128)S(1)}, f32[1,160,2,640]{3,2,1,0:T(2,128)}, u32[]{:S(2)}) copy-start(f32[1,160,2,640]{3,2,1,0:T(2,128)} %param.11) | copy-start | bytes 2457604
  215.3 101.7 %all-gather.27.cloned.1.call-start = ((), (), s32[]{:S(2)}) async-start(), calls=%async_computation.10 | async-start | bytes 4096000 | tf_op jit(solution)/shard_map/all_gather | solution.py:28
  217.3 141.7 %all-gather.11.cloned.1.call-start = ((), (), s32[]{:S(2)}) async-start(), calls=%async_computation.2 | async-start | bytes 4096000 | tf_op jit(solution)/shard_map/all_gather | solution.py:53
  328.0 67.1 %all-gather.13.cloned.1.call-start = ((), (), s32[]{:S(2)}) async-start(), calls=%async_computation.3 | async-start | bytes 4096000 | tf_op jit(solution)/shard_map/all_gather | solution.py:55
  365.6 34.8 %copy-start.3 = (f32[160,2,640]{2,0,1:T(8,128)S(1)}, f32[160,2,640]{2,0,1:T(8,128)}, u32[]{:S(2)}) copy-start(f32[160,2,640]{2,0,1:T(8,128)} %divide_bitcast_fusion) | copy-start | bytes 2457604
  365.7 68.0 %all-gather.15.cloned.1.call-start = ((), (), s32[]{:S(2)}) async-start(), calls=%async_computation.4 | async-start | bytes 4096000 | tf_op jit(solution)/shard_map/all_gather | solution.py:53
  395.1 5.4 copy-start.4
  404.2 65.4 %all-gather.17.cloned.1.call-start = ((), (), s32[]{:S(2)}) async-start(), calls=%async_computation.5 | async-start | bytes 4096000 | tf_op jit(solution)/shard_map/all_gather | solution.py:55
  440.2 34.7 %copy-start.5 = (f32[640,2,640]{2,0,1:T(8,128)S(1)}, f32[640,2,640]{2,0,1:T(8,128)}, u32[]{:S(2)}) copy-start(f32[640,2,640]{2,0,1:T(8,128)} %all-gather.15.cloned.1.call-done) | copy-start | bytes 9830404
  440.2 67.9 %all-gather.19.cloned.1.call-start = ((), (), s32[]{:S(2)}) async-start(), calls=%async_computation.6 | async-start | bytes 4096000 | tf_op jit(solution)/shard_map/all_gather | solution.py:53
  469.6 5.3 copy-start.8
  478.6 65.4 %all-gather.21.cloned.1.call-start = ((), (), s32[]{:S(2)}) async-start(), calls=%async_computation.7 | async-start | bytes 4096000 | tf_op jit(solution)/shard_map/all_gather | solution.py:55
  514.6 34.7 %copy-start.6 = (f32[640,2,640]{2,0,1:T(8,128)S(1)}, f32[640,2,640]{2,0,1:T(8,128)}, u32[]{:S(2)}) copy-start(f32[640,2,640]{2,0,1:T(8,128)} %all-gather.19.cloned.1.call-done) | copy-start | bytes 9830404
  514.6 67.9 %all-gather.23.cloned.1.call-start = ((), (), s32[]{:S(2)}) async-start(), calls=%async_computation.8 | async-start | bytes 4096000 | tf_op jit(solution)/shard_map/all_gather | solution.py:53
  544.1 5.3 copy-start.9
  553.1 36.9 %copy-start.14 = (f32[1,2,640,256]{3,2,1,0:T(8,128)S(1)}, f32[1,2,640,256]{3,2,1,0:T(8,128)}, u32[]{:S(2)}) copy-start(f32[1,2,640,256]{3,2,1,0:T(8,128)} %param.15) | copy-start | bytes 3932164
  553.1 97.7 %all-gather.25.cloned.1.call-start = ((), (), s32[]{:S(2)}) async-start(), calls=%async_computation.9 | async-start | bytes 4096000 | tf_op jit(solution)/shard_map/all_gather | solution.py:55
  591.5 6.0 copy-start.1
  597.5 5.7 copy-start.11
  597.5 5.8 copy-start.12
  597.5 5.8 copy-start.13
  612.9 36.4 %all-to-all-start = ((f32[2,8,80,256]{3,2,0,1:T(8,128)}), f32[2,8,80,256]{3,2,0,1:T(8,128)S(1)}, u32[]{:S(2)}, u32[]{:S(2)}) async-start(f32[2,8,80,256]{3,2,0,1:T(8,128)} %copy_select_fusion), calls=%async_computation | async-start | bytes 2621440 | tf_op jit(solution)/shard_map/all_to_all | solution.py:67
  650.8 5.3 copy-start.2
  650.8 5.4 copy-start.7
Sparse Core Ops, SparseCore 0:
  13.0 186.0 all-reduce.3
  215.4 69.4 all-reduce.5
  287.1 29.9 all-gather.26
  328.1 30.9 all-gather.10
  365.8 29.2 all-gather.12
  404.3 29.2 all-gather.14
  440.3 29.2 all-gather.16
  478.8 29.2 all-gather.18
  514.8 29.2 all-gather.20
  553.2 29.2 all-gather.22
  589.2 29.3 all-gather.24
where the time goes:
time: 676 us; the launch traced here: 668 us
  waiting for transfers between devices  519 us (77%)
  matrix products  86.3 us (13%)
  local copies, waits for them, and re-layouts  23.3 us (3%)
  between operations  15.3 us (2%)
  other arithmetic  11.5 us (2%)
  starting transfers between devices  6.88 us (1%)
    psum x1, waiting for transfers between devices, body(): summed = lax.psum(local, 'dp')  185 us
    all_gather x4, waiting for transfers between devices, body(): gathered = lax.all_gather(iterate, 'mp', axis=0, tiled=True)  119 us
    all_gather x4, waiting for transfers between devices, body(): inner_whole = lax.all_gather(inner, 'mp', axis=0, tiled=True)  87.5 us
    unnamed x12, waiting for transfers between devices  66.2 us
    all_to_all x1, waiting for transfers between devices, body(): lax.all_to_all(sending, 'dp', split_axis=1, concat_axis=0, tiled=True)  30.8 us
    all_gather x1, waiting for transfers between devices, body(): complete_eigvectors = lax.all_gather(basis[0], 'mp', axis=0, tiled=True)  30.1 us
    dot_general x4, matrix products, body(): jnp.einsum('rsf,esf->rse', iterate, gathered, precision=top_precision)  26.1 us
    dot_general x4, matrix products, body(): jnp.einsum('rse,esg->rsg', inner, inner_whole, precision=top_precision)  21.2 us
  transfers between devices with their start and end apart: 12, of which 11 were waited for; matrix products, arithmetic and copies ran while one was open for 4% of the time, Pallas kernels for 0%

commit v1 on v0

v1 whole, which is shorter than its diff:
```python
import jax
import jax.numpy as jnp
from jax import lax
from jax.experimental import pallas as pl
from jax.experimental.pallas import tpu as pltpu
from jax.sharding import PartitionSpec as P

NS_ITERS = 4
BF = jnp.bfloat16
F32 = jnp.float32


def halves(x):
    hi = x.astype(BF)
    return hi, (x - hi.astype(F32)).astype(BF)


def product(a, b, dims):
    (ah, al), (bh, bl) = a, b

    def dot(p, q):
        return lax.dot_general(p, q, (dims, ((), ())), preferred_element_type=F32)

    return dot(ah, bh) + (dot(ah, bl) + dot(al, bh))


NN = ((1,), (0,))
NT = ((1,), (1,))
TN = ((0,), (0,))


def weights_kernel(chosen_ref, basis_ref, grad_ref, m1_ref, m2_ref, master_ref, out_ref, work_ref):
    basis = halves(basis_ref[0])
    turned = product(basis, halves(grad_ref[0]), TN)
    first = 0.9 * m1_ref[0] + 0.1 * turned
    second = 0.95 * m2_ref[0] + 0.05 * turned * turned
    direction = product(basis, halves(first / (jnp.sqrt(second) + 1e-08)), NN)
    held = master_ref[0]
    groups, block_rows = out_ref.shape[1:3]
    slot = pl.program_id(0)
    if block_rows % 8:
        out_ref[0] = (held - 0.1 * (direction + 0.1 * held)).reshape(out_ref.shape[1:])
        return
    work_ref[...] = held - 0.1 * (direction + 0.1 * held)
    for g in range(groups):
        start = pl.multiple_of(chosen_ref[slot, g] * block_rows, 8)
        out_ref[0, g] = work_ref[pl.ds(start, block_rows), :]


def new_weights(chosen, basis, grad, m1, m2, master):
    slots, d, c = grad.shape
    groups = chosen.shape[1]
    if (d // groups) % 8:
        whole = weights_call(chosen, basis, grad, m1, m2, master, (slots, 1, d, c))
        whole = whole.reshape(slots, groups, d // groups, c)
        pick = lambda s, g: lax.dynamic_index_in_dim(whole[s], chosen[s, g], 0, keepdims=False)
        return jnp.stack([jnp.stack([pick(s, g) for g in range(groups)]) for s in range(slots)])
    return weights_call(chosen, basis, grad, m1, m2, master, (slots, groups, d // groups, c))


def weights_call(chosen, basis, grad, m1, m2, master, out_shape):
    slots, d, c = grad.shape
    wide = pl.BlockSpec((1, d, c), lambda i: (i, 0, 0))
    return pl.pallas_call(
        weights_kernel,
        grid=(slots,),
        out_shape=jax.ShapeDtypeStruct(out_shape, F32),
        in_specs=[
            pl.BlockSpec(memory_space=pltpu.SMEM),
            pl.BlockSpec((1, d, d), lambda i: (i, 0, 0)),
            wide,
            wide,
            wide,
            wide,
        ],
        out_specs=pl.BlockSpec((1,) + out_shape[1:], lambda i: (i, 0, 0, 0)),
        scratch_shapes=[pltpu.VMEM((d, c), F32)],
        cost_estimate=pl.CostEstimate(
            flops=12 * slots * d * d * c, bytes_accessed=4 * slots * (d * d + 5 * d * c), transcendentals=0
        ),
        compiler_params=pltpu.CompilerParams(vmem_limit_bytes=48 * 2**20),
        name="weights",
    )(chosen, basis, grad, m1, m2, master)


def refresh_kernel(grad_ref, factor_ref, basis_ref, out_ref):
    d = basis_ref.shape[0]
    outer = jnp.zeros((d, d), F32)
    for j in range(grad_ref.shape[0]):
        g = halves(grad_ref[j])
        outer = outer + product(g, g, NT)
    statistic = 0.95 * factor_ref[...] + 0.05 * outer
    power = product(halves(statistic), halves(basis_ref[...]), NN)
    out_ref[...] = power / jnp.sqrt(jnp.sum(power * power) + 1e-06)

    @pl.loop(0, NS_ITERS)
    def _(step):
        x = out_ref[...]
        xs = halves(x)
        inner = product(xs, xs, NT)
        ins = halves(inner)
        merged = -4.775 * inner + 2.0315 * product(ins, ins, NN)
        out_ref[...] = 3.4445 * x + product(halves(merged), xs, NN)


def refresh(grad, factor, basis):
    d = basis.shape[0]
    return pl.pallas_call(
        refresh_kernel,
        out_shape=jax.ShapeDtypeStruct((d, d), F32),
        in_specs=[pl.BlockSpec(memory_space=pltpu.VMEM)] * 3,
        out_specs=pl.BlockSpec(memory_space=pltpu.VMEM),
        cost_estimate=pl.CostEstimate(flops=90 * d**3, bytes_accessed=4 * 6 * d * d, transcendentals=0),
        compiler_params=pltpu.CompilerParams(vmem_limit_bytes=56 * 2**20),
        name="refresh",
    )(grad, factor, basis)


def body(partials, owner, rowblock, factor, basis, moment1, moment2, master):
    groups = lax.axis_size("dp")
    parts = lax.axis_size("mp")
    my_index = lax.axis_index("dp")
    mine = lax.axis_index("mp")
    count = owner.shape[0]
    rows, slots, d = factor.shape[1:]
    order = jnp.arange(count)
    same = owner[:, None] == owner[None, :]
    slot = jnp.sum((same & (order[None, :] < order[:, None])).astype(jnp.int32), axis=1)
    hits = (owner[None, :] == my_index) & (slot[None, :] == jnp.arange(slots)[:, None])
    valid = jnp.any(hits, axis=1)
    my_matrix = jnp.sum(hits.astype(jnp.int32) * order[None, :], axis=1)

    basis_all = lax.all_gather(jnp.swapaxes(basis[0], 0, 1), "mp", axis=0)
    factor_all = lax.all_gather(jnp.swapaxes(factor[0], 0, 1), "mp", axis=0)

    summed = lax.psum(partials[0].astype(F32), "dp")
    grad = jnp.stack(
        [
            jnp.where(valid[s], lax.dynamic_index_in_dim(summed, my_matrix[s], 0, keepdims=False), 0.0)
            for s in range(slots)
        ]
    ) * (1.0 / groups)

    whole_basis = jnp.swapaxes(basis_all, 0, 1).reshape(slots, d, d)
    chosen = jnp.stack(
        [lax.dynamic_index_in_dim(rowblock, my_matrix[s], 0, keepdims=False) for s in range(slots)]
    )
    sending = new_weights(chosen, whole_basis, grad, moment1[0], moment2[0], master[0])
    grad_all = lax.all_gather(grad, "mp", axis=0)

    my_slot = mine % slots
    take = lambda a: lax.dynamic_index_in_dim(a, my_slot, 1, keepdims=False)
    iterate = refresh(
        take(grad_all),
        take(factor_all).reshape(d, d),
        lax.dynamic_index_in_dim(whole_basis, my_slot, 0, keepdims=False),
    )
    iterate = jnp.where(valid[my_slot], iterate, 0.0).reshape(parts, rows, d)
    block = lambda i: lax.dynamic_index_in_dim(iterate, i, 0, keepdims=False)
    base = mine - my_slot
    pieces = [block(mine)]
    for off in range(1, slots):
        pairs = [(i, i // slots * slots + (i + off) % slots) for i in range(parts)]
        pieces.append(lax.ppermute(block(base + (my_slot + off) % slots), "mp", pairs))
    stacked = jnp.stack(pieces)
    new_basis = jnp.stack(
        [lax.dynamic_index_in_dim(stacked, (my_slot - s) % slots, 0, keepdims=False) for s in range(slots)], axis=1
    )[None]

    received = lax.all_to_all(sending, "dp", split_axis=1, concat_axis=0, tiled=True)
    place = owner * slots + slot
    train_weights = jnp.stack(
        [lax.dynamic_index_in_dim(received, place[m], 0, keepdims=False) for m in range(count)]
    )
    return (train_weights, new_basis)


def solution(mesh):
    placed = (
        P("dp", None, None, "mp"),
        P(),
        P(),
        P("dp", "mp", None, None),
        P("dp", "mp", None, None),
        P("dp", None, None, "mp"),
        P("dp", None, None, "mp"),
        P("dp", None, None, "mp"),
    )
    return jax.shard_map(
        body,
        mesh=mesh,
        in_specs=placed,
        out_specs=(P(None, "dp", None, "mp"), P("dp", "mp", None, None)),
        check_vma=False,
    )
```

time: 676 us -> 319 us (0.47); the launches traced: 668 us -> 318 us
  waiting for transfers between devices: 519 us -> 188 us
  matrix products: 86.3 us -> 0 us
  Pallas kernels: 0 us -> 47.8 us
  between operations: 15.3 us -> 34.7 us
    all_gather x9 -> x3, waiting for transfers between devices: 237 us -> 0.03 us  [the longest x1 0.02 us: body(): basis_all = lax.all_gather(jnp.swapaxes(basis[0], 0, 1), 'mp', axis=0)]
    dot_general x17 -> x0, matrix products: 86.3 us -> none  [the longest x4 26.1 us: body(): jnp.einsum('rsf,esf->rse', iterate, gathered, precision=top_precision)]
    unnamed x12 -> x4, waiting for transfers between devices: 66.2 us -> 0.07 us
    pallas_call x0 -> x2, Pallas kernels: none -> 47.8 us  [the longest x1 39.1 us: refresh(): pl.pallas_call(refresh_kernel, out_shape=jax.ShapeDtypeStruct((d, d), F32...]
    all_to_all x1, waiting for transfers between devices: 30.8 us -> 10.9 us  [body(): lax.all_to_all(sending, 'dp', split_axis=1, concat_axis=0, tiled=True)]
    psum x1, waiting for transfers between devices: 185 us -> 177 us  [body(): summed = lax.psum(partials[0].astype(F32), 'dp')]
  transfers between devices with their start and end apart: 12 -> 6, of which waited for: 11 -> 2; matrix products, arithmetic and copies ran while one was open for 4% -> 8% of each run, Pallas kernels for 0% -> 3%
where the time goes in v1:
time: 319 us; the launch traced here: 318 us
  waiting for transfers between devices  188 us (59%)
  Pallas kernels  47.8 us (15%)
  between operations  34.7 us (11%)
  local copies, waits for them, and re-layouts  28.2 us (9%)
  other arithmetic  13 us (4%)
  starting transfers between devices  6.3 us (2%)
    psum x1, waiting for transfers between devices, body(): summed = lax.psum(partials[0].astype(F32), 'dp')  177 us
    pallas_call x1, Pallas kernels, refresh(): pl.pallas_call(refresh_kernel, out_shape=jax.ShapeDtypeStruct((d, d), F32...  39.1 us
    unnamed x23, local copies, waits for them, and re-layouts  11.2 us
    all_to_all x1, waiting for transfers between devices, body(): lax.all_to_all(sending, 'dp', split_axis=1, concat_axis=0, tiled=True)  10.9 us
    pallas_call x1, Pallas kernels, weights_call(): pl.pallas_call(weights_kernel, grid=(slots,), out_shape=jax.ShapeDtypeStr...  8.69 us
  transfers between devices with their start and end apart: 6, of which 2 were waited for; matrix products, arithmetic and copies ran while one was open for 8% of the time, Pallas kernels for 3%

profile of v1, /device:TPU:1, one launch (start us, length us, event | category | flops | bytes accessed | tf_op | source)
XLA Modules:
  0.0 318.3 jit_solution(15269110245269388024)
XLA Ops:
  8.0 0.0 all-reduce.2.cloned.1.call-start
  8.0 4.6 %bitcast_convert_fusion = f32[8,640,256]{2,1,0:T(8,128)} fusion(bf16[1,8,640,256]{3,2,1,0:T(8,128)(2,1)} %param.8), kind=kLoop, calls=%fused_computation | loop fusion | flops 1310720 | bytes 7864320 | tf_op jit(solution)/shard_map/convert_element_type | solution.py:136
  12.7 0.0 all-gather.8.cloned.1.call-start
  12.7 1.1 copy-done.3
  13.8 0.9 copy.32
  14.7 0.0 all-gather.8.cloned.1.call-update
  14.8 0.0 all-gather.10.cloned.1.call-start
  14.8 1.0 copy.31
  15.8 0.0 all-gather.6.cloned.1.call-start
  15.9 0.2 convert_reduce_fusion
  16.1 0.1 select_reduce_fusion
  16.2 0.7 fusion.6
  20.7 0.1 fusion.3
  20.8 0.7 fusion.4
  21.5 177.4 %all-reduce.2.cloned.1.call-done = f32[8,640,256]{2,1,0:T(8,128)} async-done(((f32[8,640,256]{2,1,0:T(8,128)}), f32[8,640,256]{2,1,0:T(8,128)}) %all-reduce.2.cloned.1.call-update) | async-done | bytes 5242896 | tf_op jit(solution)/shard_map/psum | solution.py:136
  198.9 2.7 dynamic-slice_select_fusion.1
  201.6 1.2 maximum_multiply_fusion.1
  202.8 0.8 constant_dynamic-slice_fusion.3
  203.5 0.0 all-gather.8.cloned.1.call-done
  203.6 3.8 %copy.23 = f32[4,2,160,640]{3,2,0,1:T(8,128)} copy(f32[4,2,160,640]{3,2,1,0:T(8,128)} %bitcast.62) | data formatting | bytes 6553600 | tf_op jit(solution)/shard_map/all_gather | solution.py:133
  207.4 0.1 maximum_multiply_fusion.grad_ref
  207.5 1.4 copy-done
  208.9 0.5 copy-done.1
  209.4 8.7 %weights.1 = f32[2,8,80,256]{3,2,1,0:T(8,128)S(1)} custom-call(s32[2,8]{1,0:T(2,128)S(1)} %pad_add_fusion.chosen_ref, f32[2,640,640]{2,1,0:T(8,128)} %bitcast.57, f32[2,640,256]{2,1,0:T(8,128)S(1)} %maximum_multiply_fusion.grad_ref, f32[2,640,256]{2,1,0:T(8,128)S(1)} %bitcast.55, f32[2,640,256]{2,1,0:T(8,128)S(1)} %bitcast.56, f32[2,640,256]{2,1,0:T(8,128)} %bitcast.66), custom_call_target="tpu_custom_call" | custom-call | flops 2516582400 | bytes 9830400 | tf_op jit(solution)/shard_map/weights/pallas_call | solution.py:64
  218.1 1.2 copy.24
  219.3 4.6 %all-to-all-start = ((f32[2,8,80,256]{3,2,0,1:T(8,128)}), f32[2,8,80,256]{3,2,0,1:T(8,128)}, u32[]{:S(2)}, u32[]{:S(2)}) async-start(f32[2,8,80,256]{3,2,0,1:T(8,128)} %copy.24), calls=%async_computation | async-start | bytes 2621440 | tf_op jit(solution)/shard_map/all_to_all | solution.py:170
  223.9 0.7 fusion.5
  239.6 1.3 dynamic-slice_bitcast_fusion.1.basis_ref
  240.9 2.8 constant_dynamic-slice_fusion.1
  243.7 10.9 %all-to-all-done = f32[2,8,80,256]{3,2,0,1:T(8,128)} async-done(((f32[2,8,80,256]{3,2,0,1:T(8,128)}), f32[2,8,80,256]{3,2,0,1:T(8,128)}, u32[]{:S(2)}, u32[]{:S(2)}) %all-to-all-start) | async-done | bytes 1310752 | tf_op jit(solution)/shard_map/all_to_all | solution.py:170
  254.6 0.9 dynamic-slice_dynamic-update-slice_fusion.7
  255.5 0.9 dynamic-slice_dynamic-update-slice_fusion.6
  256.4 0.9 dynamic-slice_dynamic-update-slice_fusion.5
  257.3 0.9 dynamic-slice_dynamic-update-slice_fusion.4
  258.2 3.5 %dynamic-slice_bitcast_fusion.grad_ref = f32[4,640,256]{2,1,0:T(8,128)} fusion(f32[4,2,640,256]{3,2,1,0:T(8,128)} %all-gather.6.cloned.1.call-done, s32[]{:T(128)S(6)} %select_n.116), kind=kLoop, calls=%fused_computation.1 | loop fusion | bytes 5242884 | tf_op jit(solution)/shard_map/jit(dynamic_index_in_dim)/squeeze | solution.py:152
  261.7 39.1 %refresh.1 = f32[640,640]{1,0:T(8,128)} custom-call(f32[4,640,256]{2,1,0:T(8,128)} %dynamic-slice_bitcast_fusion.grad_ref, f32[640,640]{1,0:T(8,128)} %bitcast.65, f32[640,640]{1,0:T(8,128)} %dynamic-slice_bitcast_fusion.1.basis_ref), custom_call_target="tpu_custom_call" | custom-call | flops 23592960000 | bytes 9830400 | tf_op jit(solution)/shard_map/refresh/pallas_call | solution.py:108
  300.8 2.2 broadcast_select_fusion
  303.0 0.1 dynamic-slice_bitcast_fusion.2
  303.1 1.6 collective-permute-start
  304.7 0.9 dynamic-slice_dynamic-update-slice_fusion.3
  305.5 0.9 dynamic-slice_dynamic-update-slice_fusion.2
  306.4 0.9 dynamic-slice_dynamic-update-slice_fusion.1
  307.3 0.9 dynamic-slice_dynamic-update-slice_fusion
  308.2 0.2 fusion.1
  308.4 0.3 stack.52
  308.7 0.3 stack.51
  309.0 0.1 copy-done.5
  309.1 1.6 maximum_bitcast_fusion
  (19 shorter events, 0.1 us)
Async XLA Ops:
  8.0 190.9 %all-reduce.2.cloned.1.call-start = ((), (), s32[]{:S(2)}) async-start(), calls=%async_computation.1 | async-start | bytes 10485760 | tf_op jit(solution)/shard_map/psum | solution.py:136
  12.6 1.1 copy-start.3
  12.7 2.2 copy-start.4
  12.7 190.9 %all-gather.8.cloned.1.call-start = ((), (), s32[]{:S(2)}) async-start(), calls=%async_computation.3 | async-start | bytes 4096000 | tf_op jit(solution)/shard_map/all_gather | solution.py:133
  14.7 1.1 copy-start.6
  14.8 226.2 %all-gather.10.cloned.1.call-start = ((), (), s32[]{:S(2)}) async-start(), calls=%async_computation.4 | async-start | bytes 4096000 | tf_op jit(solution)/shard_map/all_gather | solution.py:134
  15.8 242.3 %all-gather.6.cloned.1.call-start = ((), (), s32[]{:S(2)}) async-start(), calls=%async_computation.2 | async-start | bytes 6553600 | tf_op jit(solution)/shard_map/all_gather | solution.py:149
  207.4 1.5 copy-start
  207.4 2.0 copy-start.1
  218.1 21.5 %copy-start.2 = (f32[4,2,160,640]{3,2,0,1:T(8,128)S(1)}, f32[4,2,160,640]{3,2,0,1:T(8,128)}, u32[]{:S(2)}) copy-start(f32[4,2,160,640]{3,2,0,1:T(8,128)} %copy.23) | copy-start | bytes 9830404
  219.3 35.2 %all-to-all-start = ((f32[2,8,80,256]{3,2,0,1:T(8,128)}), f32[2,8,80,256]{3,2,0,1:T(8,128)}, u32[]{:S(2)}, u32[]{:S(2)}) async-start(f32[2,8,80,256]{3,2,0,1:T(8,128)} %copy.24), calls=%async_computation | async-start | bytes 2621440 | tf_op jit(solution)/shard_map/all_to_all | solution.py:170
  303.1 5.1 %collective-permute-start = (f32[160,640]{1,0:T(8,128)S(1)}, f32[160,640]{1,0:T(8,128)S(1)}, u32[]{:S(2)}, u32[]{:S(2)}) collective-permute-start(f32[160,640]{1,0:T(8,128)S(1)} %get-tuple-element.10), channel_id=1, source_target_pairs={{0,1},{1,0},{2,3},{3,2},{4,5},{5,4},{6,7},{7,6},{8,9},{9,8},{10,11... | collective-permute-start | bytes 1228808 | tf_op jit(solution)/shard_map/ppermute | solution.py:164
  308.2 0.8 copy-start.5
Sparse Core Ops, SparseCore 0:
  12.8 186.0 all-reduce.1
Sparse Core Ops, SparseCore 1:
  15.3 31.6 all-gather.7
  48.4 29.1 all-gather.9
  202.8 39.7 all-gather.5

commit v2 on v1

--- a/solution.py
+++ b/solution.py
@@ -133,13 +133,26 @@
     basis_all = lax.all_gather(jnp.swapaxes(basis[0], 0, 1), "mp", axis=0)
     factor_all = lax.all_gather(jnp.swapaxes(factor[0], 0, 1), "mp", axis=0)
 
-    summed = lax.psum(partials[0].astype(F32), "dp")
-    grad = jnp.stack(
-        [
-            jnp.where(valid[s], lax.dynamic_index_in_dim(summed, my_matrix[s], 0, keepdims=False), 0.0)
-            for s in range(slots)
-        ]
-    ) * (1.0 / groups)
+    local = partials[0].astype(F32) * (1.0 / groups)
+    pick = lambda a, m, ok: jnp.where(ok, lax.dynamic_index_in_dim(a, m, 0, keepdims=False), 0.0)
+
+    def whole_sum():
+        summed = lax.psum(local, "dp")
+        return jnp.stack([pick(summed, my_matrix[s], valid[s]) for s in range(slots)])
+
+    def owners_sum():
+        units = []
+        for g in range(groups):
+            hit = (owner == g) & (slot == 0)
+            units.append(pick(local, jnp.sum(hit * order), jnp.any(hit)))
+        lead = lax.psum_scatter(jnp.stack(units), "dp", scatter_dimension=0)
+        second = lax.psum(pick(local, jnp.sum((slot == 1) * order), jnp.any(slot == 1)), "dp")
+        return jnp.stack([lead, jnp.where(valid[1], second, 0.0)])
+
+    if groups <= count and slots == 2:
+        grad = lax.cond(jnp.sum(slot == 1) <= 1, owners_sum, whole_sum)
+    else:
+        grad = whole_sum()
 
     whole_basis = jnp.swapaxes(basis_all, 0, 1).reshape(slots, d, d)
     chosen = jnp.stack(

time: 319 us -> 397 us (1.24)
  waiting for transfers between devices: 188 us -> 235 us
  loops' own time: 0 us -> 17.1 us
  other arithmetic: 13 us -> 25.3 us
    reduce_scatter x0 -> x1, waiting for transfers between devices: none -> 107 us  [owners_sum(): lead = lax.psum_scatter(jnp.stack(units), 'dp', scatter_dimension=0)]
    psum x1, waiting for transfers between devices: 177 us -> 73 us  [owners_sum(): lax.psum(pick(local, jnp.sum((slot == 1) * order), jnp.any(slot == 1)), '...]
    all_gather x1, waiting for transfers between devices: 0.02 us -> 24.5 us  [body(): basis_all = lax.all_gather(jnp.swapaxes(basis[0], 0, 1), 'mp', axis=0)]
    all_gather x1, waiting for transfers between devices: 0.01 us -> 18.9 us  [body(): grad_all = lax.all_gather(grad, 'mp', axis=0)]
    another operation x0 -> x1, loops' own time: none -> 17.1 us  [body(): grad = lax.cond(jnp.sum(slot == 1) <= 1, owners_sum, whole_sum)]
    cond x0 -> x7, other arithmetic: none -> 9.38 us
    convert_element_type x1 -> x0, other arithmetic: 4.59 us -> none  [body(): summed = lax.psum(partials[0].astype(F32), 'dp')]
    another operation x0 -> x3, other arithmetic: none -> 4 us  [the longest x1 2.15 us: owners_sum(): lead = lax.psum_scatter(jnp.stack(units), 'dp', scatter_dimension=0)]
  transfers between devices with their start and end apart: 6 -> 7, of which waited for: 2 -> 5; matrix products, arithmetic and copies ran while one was open for 8% -> 5% of each run, Pallas kernels for 3% -> 2%
where the time goes in v2:
time: 397 us; the launch traced here: 396 us
  waiting for transfers between devices  235 us (59%)
  Pallas kernels  47.4 us (12%)
  between operations  36 us (9%)
  local copies, waits for them, and re-layouts  28.4 us (7%)
  other arithmetic  25.3 us (6%)
  loops' own time  17.1 us (4%)
  starting transfers between devices  7.28 us (2%)
    reduce_scatter x1, waiting for transfers between devices, owners_sum(): lead = lax.psum_scatter(jnp.stack(units), 'dp', scatter_dimension=0)  107 us
    psum x1, waiting for transfers between devices, owners_sum(): lax.psum(pick(local, jnp.sum((slot == 1) * order), jnp.any(slot == 1)), '...  73 us
    pallas_call x1, Pallas kernels, refresh(): pl.pallas_call(refresh_kernel, out_shape=jax.ShapeDtypeStruct((d, d), F32...  39.1 us
    all_gather x1, waiting for transfers between devices, body(): basis_all = lax.all_gather(jnp.swapaxes(basis[0], 0, 1), 'mp', axis=0)  24.5 us
    all_gather x1, waiting for transfers between devices, body(): grad_all = lax.all_gather(grad, 'mp', axis=0)  18.9 us
    another operation x1, loops' own time, body(): grad = lax.cond(jnp.sum(slot == 1) <= 1, owners_sum, whole_sum)  17.1 us
    all_to_all x1, waiting for transfers between devices, body(): lax.all_to_all(sending, 'dp', split_axis=1, concat_axis=0, tiled=True)  9.92 us
    cond x7, other arithmetic  9.38 us
  transfers between devices with their start and end apart: 7, of which 5 were waited for; matrix products, arithmetic and copies ran while one was open for 5% of the time, Pallas kernels for 2%

profile of v2, /device:TPU:1, one launch (start us, length us, event | category | flops | bytes accessed | tf_op | source)
XLA Modules:
  0.0 396.0 jit_solution(14561868756580598387)
XLA Ops:
  8.0 0.9 convert_reduce_fusion
  8.9 0.7 broadcast_compare_fusion.1
  9.8 1.3 multiply_add_fusion
  11.1 4.6 %multiply_bitcast_fusion = f32[8,640,256]{2,1,0:T(8,128)} fusion(bf16[1,8,640,256]{3,2,1,0:T(8,128)(2,1)} %param.10), kind=kLoop, calls=%fused_computation.42 | loop fusion | flops 2621440 | bytes 7864320 | tf_op jit(solution)/shard_map/mul | solution.py:136
  16.4 0.9 copy.37
  17.4 215.3 %conditional.1 = (f32[2,640,256]{2,1,0:T(8,128)S(1)}) conditional(s32[]{:T(128)} %convert_element_type.11, (pred[2]{0:T(512)(128)(4,1)S(1)}, f32[8,640,256]{2,1,0:T(8,128)}, s32[2]{0:T(128)S(1)}) %tuple.14, (s32[8]{0:T(128)S(1)}, s32[8]{0:T(128)S(1)}, s32[8]{0:T(128)S(1)}, f32[8,640,256]{2,1,0:T(8,128)}, s32[8]{0:T(128)S(1)}, ...), branch_computations={%region_4.6_spmd, %region_6.27_spmd} | conditional | flops 2130432 | bytes 79299496 | solution.py:153
  17.4 0.8 fusion.8
  18.2 0.8 select_reduce_fusion
  36.0 2.1 select_dynamic-update-slice_fusion.7
  38.1 1.7 select_dynamic-update-slice_fusion.6
  39.8 1.8 select_dynamic-update-slice_fusion.5
  41.6 1.7 select_dynamic-update-slice_fusion.4
  43.9 0.7 select_dynamic-update-slice_fusion.2
  44.7 0.7 select_dynamic-update-slice_fusion.1
  45.4 2.1 select_dynamic-update-slice_fusion
  47.5 2.3 copy-done.7
  50.0 0.7 reduce-scatter.2.cloned.1.call-update
  51.3 73.0 %all-reduce.5.cloned.1.call-done = f32[640,256]{1,0:T(8,128)} async-done(((f32[640,256]{1,0:T(8,128)}), f32[640,256]{1,0:T(8,128)}) %all-reduce.5.cloned.1.call-update) | async-done | bytes 655376 | tf_op jit(solution)/shard_map/cond/branch_1_fun/psum | solution.py:149
  124.2 0.7 select_bitcast_fusion
  124.9 106.5 %reduce-scatter.2.cloned.1.call-done = f32[1,640,256]{2,1,0:T(8,128)} async-done(((f32[8,640,256]{2,1,0:T(8,128)}), f32[1,640,256]{2,1,0:T(8,128)}) %reduce-scatter.2.cloned.1.call-update) | async-done | bytes 655376 | tf_op jit(solution)/shard_map/cond/branch_1_fun/reduce_scatter | solution.py:148
  231.4 1.2 pad_maximum_fusion.1
  233.3 0.9 copy.36
  234.8 0.6 fusion.17
  239.4 0.8 constant_dynamic-slice_fusion.3
  240.2 24.5 %all-gather.7.cloned.1.call-done = f32[8,160,640]{2,1,0:T(8,128)} async-done(((f32[2,160,640]{2,1,0:T(8,128)}), f32[8,160,640]{2,1,0:T(8,128)}) %all-gather.7.cloned.1.call-update) | async-done | bytes 3276816 | tf_op jit(solution)/shard_map/all_gather | solution.py:133
  264.8 4.1 %copy.26 = f32[4,2,160,640]{3,2,0,1:T(8,128)} copy(f32[4,2,160,640]{3,2,1,0:T(8,128)} %bitcast.68) | data formatting | bytes 6553600 | tf_op jit(solution)/shard_map/all_gather | solution.py:133
  268.8 8.3 %weights.1 = f32[2,8,80,256]{3,2,1,0:T(8,128)S(1)} custom-call(s32[2,8]{1,0:T(2,128)S(1)} %pad_add_fusion.chosen_ref, f32[2,640,640]{2,1,0:T(8,128)} %bitcast.65, f32[2,640,256]{2,1,0:T(8,128)S(1)} %copy-done.6, f32[2,640,256]{2,1,0:T(8,128)S(1)} %bitcast.62, f32[2,640,256]{2,1,0:T(8,128)S(1)} %bitcast.63, f32[2,640,256]{2,1,0:T(8,128)S(1)} %bitcast.64), custom_call_target="tpu_custom_call" | custom-call | flops 2516582400 | bytes 9830400 | tf_op jit(solution)/shard_map/weights/pallas_call | solution.py:64
  277.1 1.2 copy.27
  278.3 5.4 %all-to-all-start = ((f32[2,8,80,256]{3,2,0,1:T(8,128)}), f32[2,8,80,256]{3,2,0,1:T(8,128)}, u32[]{:S(2)}, u32[]{:S(2)}) async-start(f32[2,8,80,256]{3,2,0,1:T(8,128)} %copy.27), calls=%async_computation.1 | async-start | bytes 2621440 | tf_op jit(solution)/shard_map/all_to_all | solution.py:183
  283.7 0.7 fusion.16
  294.8 0.7 dynamic_slice.105
  300.6 1.3 dynamic-slice_bitcast_fusion.1.basis_ref
  302.0 2.9 constant_dynamic-slice_fusion.1
  304.8 9.9 %all-to-all-done = f32[2,8,80,256]{3,2,0,1:T(8,128)} async-done(((f32[2,8,80,256]{3,2,0,1:T(8,128)}), f32[2,8,80,256]{3,2,0,1:T(8,128)}, u32[]{:S(2)}, u32[]{:S(2)}) %all-to-all-start) | async-done | bytes 1310752 | tf_op jit(solution)/shard_map/all_to_all | solution.py:183
  314.8 0.9 dynamic-slice_dynamic-update-slice_fusion.7
  315.7 0.9 dynamic-slice_dynamic-update-slice_fusion.6
  316.6 0.9 dynamic-slice_dynamic-update-slice_fusion.5
  317.4 0.9 dynamic-slice_dynamic-update-slice_fusion.4
  318.3 18.9 %all-gather.9.cloned.1.call-done = f32[8,640,256]{2,1,0:T(8,128)} async-done(((f32[2,640,256]{2,1,0:T(8,128)}), f32[8,640,256]{2,1,0:T(8,128)}) %all-gather.9.cloned.1.call-update) | async-done | bytes 5242896 | tf_op jit(solution)/shard_map/all_gather | solution.py:162
  337.2 3.5 dynamic-slice_bitcast_fusion.grad_ref
  340.7 39.1 %refresh.1 = f32[640,640]{1,0:T(8,128)} custom-call(f32[4,640,256]{2,1,0:T(8,128)} %dynamic-slice_bitcast_fusion.grad_ref, f32[640,640]{1,0:T(8,128)} %bitcast.71, f32[640,640]{1,0:T(8,128)} %dynamic-slice_bitcast_fusion.1.basis_ref), custom_call_target="tpu_custom_call" | custom-call | flops 23592960000 | bytes 9830400 | tf_op jit(solution)/shard_map/refresh/pallas_call | solution.py:108
  379.8 0.8 broadcast_select_fusion
  380.7 1.7 collective-permute-start
  382.4 0.9 dynamic-slice_dynamic-update-slice_fusion.3
  383.3 0.9 dynamic-slice_dynamic-update-slice_fusion.2
  384.2 0.9 dynamic-slice_dynamic-update-slice_fusion.1
  385.1 0.9 dynamic-slice_dynamic-update-slice_fusion
  386.8 1.6 maximum_bitcast_fusion
  (44 shorter events, 3.6 us)
Async XLA Ops:
  11.1 5.3 %copy-start.8 = (f32[1,160,2,640]{3,2,1,0:T(2,128)S(1)}, f32[1,160,2,640]{3,2,1,0:T(2,128)}, u32[]{:S(2)}) copy-start(f32[1,160,2,640]{3,2,1,0:T(2,128)} %param.14) | copy-start | bytes 2457604
  11.1 5.3 %copy-start.11 = (s32[8]{0:T(128)S(1)}, s32[8]{0:T(128)}, u32[]{:S(2)}) copy-start(s32[8]{0:T(128)} %param.11) | copy-start | bytes 100
  17.4 215.9 %copy-start.9 = (f32[1,160,2,640]{3,2,1,0:T(2,128)S(1)}, f32[1,160,2,640]{3,2,1,0:T(2,128)}, u32[]{:S(2)}) copy-start(f32[1,160,2,640]{3,2,1,0:T(2,128)} %param.13) | copy-start | bytes 2457604
  17.4 106.9 %all-reduce.5.cloned.1.call-start = ((), (), s32[]{:S(2)}) async-start(), calls=%async_computation.4 | async-start | bytes 1310720 | tf_op jit(solution)/shard_map/cond/branch_1_fun/psum | solution.py:149
  35.9 7.4 %copy-start.3 = (f32[8,640,256]{2,1,0:T(8,128)S(1)}, f32[8,640,256]{2,1,0:T(8,128)}, u32[]{:S(2)}) copy-start(f32[8,640,256]{2,1,0:T(8,128)} %get-tuple-element.18) | copy-start | bytes 15728644 | tf_op jit(solution)/shard_map/cond
  47.5 2.3 copy-start.7
  49.9 181.5 %reduce-scatter.2.cloned.1.call-start = ((), (), s32[]{:S(2)}) async-start(), calls=%async_computation.3 | async-start | bytes 5898240 | tf_op jit(solution)/shard_map/cond/branch_1_fun/reduce_scatter | solution.py:148
  232.6 1.7 copy-start.5
  232.6 32.1 %all-gather.7.cloned.1.call-start = ((), (), s32[]{:S(2)}) async-start(), calls=%async_computation.5 | async-start | bytes 4096000 | tf_op jit(solution)/shard_map/all_gather | solution.py:133
  233.2 68.7 %all-gather.11.cloned.1.call-start = ((), (), s32[]{:S(2)}) async-start(), calls=%async_computation.7 | async-start | bytes 4096000 | tf_op jit(solution)/shard_map/all_gather | solution.py:134
  234.2 103.0 %all-gather.9.cloned.1.call-start = ((), (), s32[]{:S(2)}) async-start(), calls=%async_computation.6 | async-start | bytes 6553600 | tf_op jit(solution)/shard_map/all_gather | solution.py:162
  264.8 4.1 %copy-start = (f32[1,2,640,256]{3,2,1,0:T(8,128)S(1)}, f32[1,2,640,256]{3,2,1,0:T(8,128)}, u32[]{:S(2)}) copy-start(f32[1,2,640,256]{3,2,1,0:T(8,128)} %param.15) | copy-start | bytes 3932164
  264.8 4.1 %copy-start.1 = (f32[1,2,640,256]{3,2,1,0:T(8,128)S(1)}, f32[1,2,640,256]{3,2,1,0:T(8,128)}, u32[]{:S(2)}) copy-start(f32[1,2,640,256]{3,2,1,0:T(8,128)} %param.16) | copy-start | bytes 3932164
  264.8 4.1 %copy-start.2 = (f32[1,2,640,256]{3,2,1,0:T(8,128)S(1)}, f32[1,2,640,256]{3,2,1,0:T(8,128)}, u32[]{:S(2)}) copy-start(f32[1,2,640,256]{3,2,1,0:T(8,128)} %param.17) | copy-start | bytes 3932164
  264.8 4.1 %copy-start.6 = (f32[2,640,256]{2,1,0:T(8,128)S(1)}, f32[2,640,256]{2,1,0:T(8,128)}, u32[]{:S(2)}) copy-start(f32[2,640,256]{2,1,0:T(8,128)} %copy-done.5) | copy-start | bytes 3932164
  277.1 23.5 %copy-start.4 = (f32[4,2,160,640]{3,2,0,1:T(8,128)S(1)}, f32[4,2,160,640]{3,2,0,1:T(8,128)}, u32[]{:S(2)}) copy-start(f32[4,2,160,640]{3,2,0,1:T(8,128)} %copy.26) | copy-start | bytes 9830404
  278.3 36.4 %all-to-all-start = ((f32[2,8,80,256]{3,2,0,1:T(8,128)}), f32[2,8,80,256]{3,2,0,1:T(8,128)}, u32[]{:S(2)}, u32[]{:S(2)}) async-start(f32[2,8,80,256]{3,2,0,1:T(8,128)} %copy.27), calls=%async_computation.1 | async-start | bytes 2621440 | tf_op jit(solution)/shard_map/all_to_all | solution.py:183
  380.7 5.3 %collective-permute-start = (f32[160,640]{1,0:T(8,128)S(1)}, f32[160,640]{1,0:T(8,128)S(1)}, u32[]{:S(2)}, u32[]{:S(2)}) collective-permute-start(f32[160,640]{1,0:T(8,128)S(1)} %get-tuple-element.77), channel_id=1, source_target_pairs={{0,1},{1,0},{2,3},{3,2},{4,5},{5,4},{6,7},{7,6},{8,9},{9,8},{10,11... | collective-permute-start | bytes 1228808 | tf_op jit(solution)/shard_map/ppermute | solution.py:177
  386.0 2.4 copy-start.10
Sparse Core Ops, SparseCore 0:
  50.0 74.1 all-reduce.4
  128.2 103.1 reduce-scatter.1
Sparse Core Ops, SparseCore 1:
  235.3 29.4 all-gather.6
  266.3 29.1 all-gather.10
  296.9 40.3 all-gather.8
